TPU v7x, 32 devices: a whole 2x2x4 slice. The times are simulated.
32 devices in a mesh: row: 16 (over z, y, core), col: 2 (over x).
Axes of the slice: x: 2, y: 2, z: 4, core: 2. Of those that a mesh axis runs over, the one named last changes fastest.
Arguments:
- kernel: bfloat16 [1312, 16, 2, 10496], P(None, 'row', 'col'), may hold values from -1 to 8, as said below
Outputs:
- factored: float32 [1312, 16, 2, 10496], P(None, 'row', 'col')
Inputs may be any that keep to these rules, and one draw needn't show every extreme that they name: kernel is symmetric (entry i, j equals entry j, i), and its leading 2 * 256 rows and columns form a positive definite matrix.
All inputs are finite; a program needn't handle non-finite values.
Results may differ from a plain program's by a relative error of at most 0.0086.
Values may be sent and summed in bfloat16 or wider, within the bound.
A program may use at most 256 MiB of HBM per device.

v0:
```python
import jax
import jax.numpy as jnp
from jax import lax
from jax.sharding import PartitionSpec as P

B = 256
STEPS = 2


def contract_last(left, right):
    return lax.dot_general(
        left, right, (((1,), (1,)), ((), ())), preferred_element_type=jnp.float32
    )


def on_device(kernel):
    row_count = lax.axis_size("row")
    col_count = lax.axis_size("col")
    row_index = lax.axis_index("row")
    col_index = lax.axis_index("col")
    rows_each = B // row_count
    cols_each = B // col_count
    work = kernel[:, 0, 0, :].astype(jnp.float32)
    eye = jnp.eye(B, dtype=jnp.float32)
    for step in range(STEPS):
        row_start = step * rows_each
        row_end = row_start + rows_each
        col_start = step * cols_each
        col_end = col_start + cols_each
        piece = work[row_start:row_end, col_start:col_end].reshape(rows_each, 1, cols_each)
        gathered = lax.all_gather(piece, ("row", "col"), axis=1, tiled=True)
        corner = jnp.transpose(
            gathered.reshape(rows_each, row_count, col_count, cols_each), (0, 1, 3, 2)
        ).reshape(B, B)
        factor = jnp.linalg.cholesky(corner)
        inverse_b = jax.scipy.linalg.solve_triangular(factor, eye, lower=True).astype(jnp.bfloat16)
        column_b = work[row_end:, col_start:col_end].astype(jnp.bfloat16)[:, :, None]
        column_all = lax.all_gather(column_b, "col", axis=2, tiled=True).reshape(-1, B)
        solved = contract_last(column_all, inverse_b)
        inverse_cube = inverse_b.reshape(B, rows_each, row_count)
        row_b = work[row_start:row_end, col_end:].astype(jnp.bfloat16)[:, None, :]
        group_rows = lax.all_gather(row_b, "row", axis=1, tiled=True)
        count = group_rows.shape[1]
        block = inverse_cube.reshape(B, rows_each * count)
        transposed = jnp.dot(
            block, group_rows.reshape(rows_each * count, -1), preferred_element_type=jnp.float32
        )
        solved_b = solved.astype(jnp.bfloat16)
        transposed_b = transposed.astype(jnp.bfloat16)
        trailing = work[row_end:, col_end:] - jnp.dot(
            solved_b, transposed_b, preferred_element_type=jnp.float32
        )
        work = work.at[row_end:, col_end:].set(trailing)
        own_rows = lax.dynamic_index_in_dim(
            factor.reshape(rows_each, row_count, cols_each, col_count), row_index, 1, keepdims=False
        )
        own_factor = lax.dynamic_index_in_dim(own_rows, col_index, 2, keepdims=False)
        own_solved = lax.dynamic_index_in_dim(
            solved.reshape(-1, cols_each, col_count), col_index, 2, keepdims=False
        )
        own_transposed = lax.dynamic_index_in_dim(
            transposed.reshape(rows_each, row_count, -1), row_index, 1, keepdims=False
        )
        work = work.at[row_start:row_end, col_start:col_end].set(own_factor)
        work = work.at[row_end:, col_start:col_end].set(own_solved)
        work = work.at[row_start:row_end, col_end:].set(own_transposed)
    return work[:, None, None, :]


def solution(mesh):
    in_specs = (P(None, "row", "col", None),)
    out_specs = P(None, "row", "col", None)
    return jax.shard_map(
        on_device, mesh=mesh, in_specs=in_specs, out_specs=out_specs, check_vma=False
    )
```

profile of v0, /device:TPU:0, one launch (start us, length us, event | category | flops | bytes accessed | tf_op | source)
XLA Modules:
  0.0 604.3 jit_solution(6643292991820192824)
XLA Ops:
  8.3 26.2 %bitcast_convert_fusion = f32[1312,10496]{1,0:T(8,128)} fusion(bf16[1312,1,1,10496]{3,0,2,1:T(8,128)(2,1)} %param.20), kind=kLoop, calls=%fused_computation.89 | loop fusion | flops 13770752 | bytes 82624512 | tf_op jit(solution)/shard_map/convert_element_type | solution.py:23
  35.2 72.0 %all-gather = f32[16,4096]{1,0:T(8,128)S(1)} all-gather(f32[16,128]{1,0:T(8,128)S(1)} %slice.268), channel_id=2, replica_groups=mesh['row'=16,'col'=2] {'row','col'}, dimensions={1}, use_global_device_ids=true | all-gather | bytes 270336 | tf_op jit(solution)/shard_map/all_gather | solution.py:31
  107.4 1.8 copy.24
  110.4 11.7 %cholesky.130 = f32[128,128]{1,0:T(8,128)S(1)} custom-call(f32[128,128]{1,0:T(8,128)S(1)} %cholesky.194), custom_call_target="Cholesky" | custom-call | tf_op jit(solution)/shard_map/jit(cholesky)/cholesky | solution.py:35
  122.2 9.8 %custom-call.13 = f32[1,128,128]{1,2,0:T(8,128)S(1)} custom-call(f32[1,128,128]{2,1,0:T(8,128)S(1)} %get-tuple-element.150), custom_call_target="InvertDiagBlocksLowerTriangular" | custom-call | tf_op jit(solution)/shard_map/jit(cholesky)/cholesky | solution.py:35
  132.5 12.1 %cholesky.147 = f32[128,128]{1,0:T(8,128)S(1)} custom-call(f32[128,128]{1,0:T(8,128)S(1)} %convolution_subtract_fusion.3), custom_call_target="Cholesky" | custom-call | tf_op jit(solution)/shard_map/jit(cholesky)/cholesky | solution.py:35
  146.6 3.8 while.12
  150.4 19.7 %custom-call.14 = f32[2,128,128]{1,2,0:T(8,128)S(1)} custom-call(f32[2,128,128]{2,1,0:T(8,128)S(1)} %get-tuple-element.117), custom_call_target="InvertDiagBlocksLowerTriangular" | custom-call | tf_op jit(solution)/shard_map/jit(_solve_triangular)/triangular_solve | solution.py:36
  171.1 7.8 %all_gather.19 = bf16[1296,128,2]{1,0,2:T(8,128)(2,1)S(1)} all-gather(bf16[1296,128,1]{1,0,2:T(8,128)(2,1)S(1)} %slice_bitcast_fusion), channel_id=1, replica_groups=mesh['row'=16,'col'=2] {'col'}, dimensions={2}, use_global_device_ids=true | all-gather | bytes 995328 | tf_op jit(solution)/shard_map/all_gather | solution.py:38
  186.6 2.0 reshape.334
  188.6 2.0 constant_dynamic-slice_fusion.6
  193.4 5.6 reshape.331
  199.0 8.1 %fusion.30 = f32[256,10368]{1,0:T(8,128)} fusion(bf16[256,10368]{1,0:T(8,128)(2,1)} %reshape.331, bf16[128,256]{1,0:T(8,128)(2,1)S(1)} %fusion.23, f32[128,256]{1,0:T(8,128)S(1)} %fusion.16), kind=kOutput, calls=%fused_computation.66 | convolution fusion | flops 1359216640 | bytes 16121856 | tf_op jit(solution)/shard_map/dot_general | solution.py:45
  207.1 37.3 %fusion = f32[1312,10496]{1,0:T(8,128)} fusion(f32[1312,10496]{1,0:T(8,128)} %bitcast_convert_fusion, f32[256,10368]{1,0:T(8,128)} %fusion.30, f32[1296,256]{1,0:T(8,128)S(1)} %convolution_bitcast_fusion), kind=kOutput, calls=%fused_computation.5 | convolution fusion | flops 6896130048 | bytes 119439360 | tf_op jit(solution)/shard_map/dot_general | solution.py:50
  244.4 3.0 constant_dynamic-slice_fusion.5
  248.9 3.2 bitcast_select_fusion
  252.1 5.7 scatter.31
  257.8 26.9 %convert.7 = bf16[1312,10496]{1,0:T(8,128)(2,1)} convert(f32[1312,10496]{1,0:T(8,128)} %scatter.31) | non-fusion elementwise | flops 13770752 | bytes 82624512 | tf_op jit(solution)/shard_map/convert.2
  287.1 66.2 %all-gather.2 = f32[16,4096]{1,0:T(8,128)S(1)} all-gather(f32[16,128]{1,0:T(8,128)S(1)} %slice.272), channel_id=4, replica_groups=mesh['row'=16,'col'=2] {'row','col'}, dimensions={1}, use_global_device_ids=true | all-gather | bytes 270336 | tf_op jit(solution)/shard_map/all_gather | solution.py:31
  353.5 1.8 copy.32
  356.5 11.7 %cholesky.164 = f32[128,128]{1,0:T(8,128)S(1)} custom-call(f32[128,128]{1,0:T(8,128)S(1)} %cholesky.197), custom_call_target="Cholesky" | custom-call | tf_op jit(solution)/shard_map/jit(cholesky)/cholesky | solution.py:35
  368.3 9.8 %custom-call.15 = f32[1,128,128]{1,2,0:T(8,128)S(1)} custom-call(f32[1,128,128]{2,1,0:T(8,128)S(1)} %get-tuple-element.146), custom_call_target="InvertDiagBlocksLowerTriangular" | custom-call | tf_op jit(solution)/shard_map/jit(cholesky)/cholesky | solution.py:35
  378.6 11.9 %cholesky.181 = f32[128,128]{1,0:T(8,128)S(1)} custom-call(f32[128,128]{1,0:T(8,128)S(1)} %convolution_subtract_fusion.2), custom_call_target="Cholesky" | custom-call | tf_op jit(solution)/shard_map/jit(cholesky)/cholesky | solution.py:35
  393.2 4.1 while.13
  397.4 20.3 %custom-call.16 = f32[2,128,128]{1,2,0:T(8,128)} custom-call(f32[2,128,128]{2,1,0:T(8,128)S(1)} %get-tuple-element.118), custom_call_target="InvertDiagBlocksLowerTriangular" | custom-call | tf_op jit(solution)/shard_map/jit(_solve_triangular)/triangular_solve | solution.py:36
  418.6 7.9 %all_gather.21 = bf16[1280,128,2]{1,0,2:T(8,128)(2,1)S(1)} all-gather(bf16[1280,128,1]{1,0,2:T(8,128)(2,1)S(1)} %slice_bitcast_fusion.1), channel_id=1, replica_groups=mesh['row'=16,'col'=2] {'col'}, dimensions={2}, use_global_device_ids=true | all-gather | bytes 983040 | tf_op jit(solution)/shard_map/all_gather | solution.py:38
  428.6 36.2 %copy.68 = f32[1312,1,1,10496]{3,0,2,1:T(8,128)} copy(f32[1312,1,1,10496]{3,0,2,1:T(8,128)} %bitcast.119) | data formatting | bytes 110166016
  473.1 5.6 reshape.344
  478.7 8.0 %fusion.28 = f32[256,10240]{1,0:T(8,128)} fusion(bf16[256,10240]{1,0:T(8,128)(2,1)} %reshape.344, bf16[128,256]{1,0:T(8,128)(2,1)S(1)} %fusion.19, f32[128,256]{1,0:T(8,128)S(1)} %fusion.14), kind=kOutput, calls=%fused_computation.64 | convolution fusion | flops 1342439424 | bytes 15925248 | tf_op jit(solution)/shard_map/dot_general | solution.py:45
  486.7 39.5 %fusion.2 = f32[1312,1,1,10496]{3,0,2,1:T(8,128)} fusion(f32[1312,1,1,10496]{3,0,2,1:T(8,128)} %copy.68, f32[1312,10496]{1,0:T(8,128)} %scatter.31, f32[256,10240]{1,0:T(8,128)} %fusion.28, f32[1280,256]{0,1:T(8,128)S(1)} %fusion.29), kind=kOutput, calls=%fused_computation.8 | convolution fusion | flops 6726942720 | bytes 116654080 | tf_op jit(solution)/shard_map/dot_general | solution.py:50
  526.1 2.9 constant_dynamic-slice_fusion.2
  531.7 65.4 %copy.38 = f32[1312,1,1,10496]{3,2,1,0:T(1,128)} copy(f32[1312,1,1,10496]{3,0,2,1:T(8,128)} %fusion.6) | data formatting | bytes 110166016 | tf_op jit(solution)/shard_map/scatter | solution.py:66
  (90 shorter events, 45.6 us)
Async XLA Ops:
  6.5 186.9 %all-gather.7.cloned.1.call-start = ((), (), s32[]{:S(2)}) async-start(), calls=%async_computation | async-start | bytes 5640192 | tf_op jit(solution)/shard_map/all_gather | solution.py:42
  8.3 464.8 %all-gather.9.cloned.1.call-start = ((), (), s32[]{:S(2)}) async-start(), calls=%async_computation.1 | async-start | bytes 5570560 | tf_op jit(solution)/shard_map/all_gather | solution.py:42
  150.4 20.7 %copy-start = (f32[256,256]{1,0:T(8,128)}, f32[256,256]{1,0:T(8,128)S(1)}, u32[]{:S(2)}) copy-start(f32[256,256]{1,0:T(8,128)S(1)} %get-tuple-element.251) | copy-start | bytes 786436
  397.3 20.3 %copy-start.1 = (f32[256,256]{1,0:T(8,128)}, f32[256,256]{1,0:T(8,128)S(1)}, u32[]{:S(2)}) copy-start(f32[256,256]{1,0:T(8,128)S(1)} %get-tuple-element.252) | copy-start | bytes 786436
Sparse Core Ops, SparseCore 0:
  9.5 59.4 all-gather.6
  286.5 52.2 all-gather.8
where the time goes:
time: 614 us; the launch traced here: 604 us
  other arithmetic  167 us (27%)
  local copies, waits for them, and re-layouts  165 us (27%)
  blocking collectives  154 us (25%)
  matrix products  102 us (17%)
  between operations  16.7 us (3%)
    all_gather x2, blocking collectives, on_device(): gathered = lax.all_gather(piece, ('row', 'col'), axis=1, tiled=True)  138 us
    dot_general x2, matrix products, on_device(): jnp.dot(solved_b, transposed_b, preferred_element_type=jnp.float32)  76.8 us
    scatter x3, local copies, waits for them, and re-layouts, on_device(): work = work.at[row_start:row_end, col_end:].set(own_transposed)  72.2 us
    another operation x13, other arithmetic, on_device(): factor = jnp.linalg.cholesky(corner)  69.2 us
    another operation x5, other arithmetic, on_device(): jax.scipy.linalg.solve_triangular(factor, eye, lower=True)  40 us
    unnamed x6, local copies, waits for them, and re-layouts  36.6 us
    another operation x3, other arithmetic  31.4 us
    convert_element_type x1, other arithmetic, on_device(): work = kernel[:, 0, 0, :].astype(jnp.float32)  26.2 us
  transfers between devices with their start and end apart: 2, of which 0 were waited for; matrix products, arithmetic and copies ran while one was open for 36% of the time, Pallas kernels for 0%

commit v1 on v0

--- a/solution.py
+++ b/solution.py
@@ -1,16 +1,296 @@
+import functools
+
 import jax
 import jax.numpy as jnp
 from jax import lax
+from jax.experimental import pallas as pl
+from jax.experimental.pallas import tpu as pltpu
 from jax.sharding import PartitionSpec as P
 
 B = 256
 STEPS = 2
+HALF = 128
+LANES = 128
+ROW_TILE = 272
+MIB = 1024 * 1024
 
 
 def contract_last(left, right):
     return lax.dot_general(
         left, right, (((1,), (1,)), ((), ())), preferred_element_type=jnp.float32
     )
+
+
+def plain_dot(left, right):
+    return jnp.dot(left, right, preferred_element_type=jnp.float32)
+
+
+def full_dot(left, right, dims=(((1,), (0,)), ((), ()))):
+    return lax.dot_general(
+        left, right, dims, precision=lax.Precision.HIGHEST, preferred_element_type=jnp.float32
+    )
+
+
+def one_hot(shape, condition):
+    i = lax.broadcasted_iota(jnp.int32, shape, 0)
+    j = lax.broadcasted_iota(jnp.int32, shape, 1)
+    return jnp.where(condition(i, j), 1.0, 0.0)
+
+
+def eliminate(block):
+    groups = HALF // 8
+    lane = lax.broadcasted_iota(jnp.int32, (8, LANES), 1)
+    sub = lax.broadcasted_iota(jnp.int32, (8, LANES), 0)
+    left = [block[8 * g:8 * g + 8, :] for g in range(groups)]
+    right = [jnp.where(lane == sub + 8 * g, 1.0, 0.0) for g in range(groups)]
+    scale = [jnp.zeros((8, LANES), jnp.float32) for _ in range(groups)]
+    for k in range(HALF):
+        g, s = divmod(k, 8)
+        row_left = jnp.broadcast_to(left[g][s:s + 1, :], (8, LANES))
+        row_right = jnp.broadcast_to(right[g][s:s + 1, :], (8, LANES))
+        pivot = jnp.broadcast_to(row_left[:, k:k + 1], (8, LANES))
+        scale[g] = jnp.where(sub == s, pivot, scale[g])
+        inverse = 1.0 / pivot
+        row_left = row_left * inverse
+        row_right = row_right * inverse
+        for u in range(g, groups):
+            if u == g and s == 7:
+                continue
+            column = jnp.broadcast_to(left[u][:, k:k + 1], (8, LANES))
+            if u == g:
+                column = jnp.where(sub > s, column, 0.0)
+            left[u] = left[u] - column * row_left
+            right[u] = right[u] - column * row_right
+    return jnp.concatenate([right[g] * lax.rsqrt(scale[g]) for g in range(groups)], axis=0)
+
+
+def factor_kernel(row_count, col_count, where_ref, diag_ref, g_rows_ref, g_cols_ref, u_rows_ref, u_cols_ref,
+                  pick_rows_ref, pick_cols_ref, corner_ref, full, work, done, table):
+    row_index, col_index = where_ref[0], where_ref[1]
+    wide = STEPS * B
+    rows_each, cols_each = B // row_count, B // col_count
+    rows_two, cols_two = wide // row_count, wide // col_count
+    gathered = jnp.concatenate(
+        [
+            jnp.concatenate([diag_ref[r * col_count + c] for r in range(row_count)], axis=0)
+            for c in range(col_count)
+        ],
+        axis=1,
+    )
+    to_rows = one_hot(
+        (wide, wide), lambda i, j: (i % row_count) * rows_two + i // row_count == j
+    ).astype(jnp.bfloat16)
+    to_cols = one_hot(
+        (wide, wide), lambda i, j: (j % col_count) * cols_two + j // col_count == i
+    ).astype(jnp.bfloat16)
+    full[...] = plain_dot(plain_dot(to_rows, gathered).astype(jnp.bfloat16), to_cols)
+    perm_rows = one_hot(
+        (B, B), lambda i, j: (j % rows_each) * row_count + j // rows_each == i
+    ).astype(jnp.bfloat16)
+    perm_cols = one_hot(
+        (B, B), lambda i, j: (j % cols_each) * col_count + j // cols_each == i
+    ).astype(jnp.bfloat16)
+    own_rows = one_hot(
+        (rows_each, B), lambda i, j: i * row_count + row_index == j
+    ).astype(jnp.bfloat16)
+    own_cols = one_hot(
+        (cols_each, B), lambda i, j: i * col_count + col_index == j
+    ).astype(jnp.bfloat16)
+
+    @pl.loop(0, STEPS)
+    def _(step):
+        here = pl.ds(pl.multiple_of(step * B, B), B)
+        work[:, :B] = full[here, here]
+        work[:, B:] = one_hot((B, B), lambda i, j: i == j)
+
+        @pl.loop(0, B // HALF)
+        def _(part):
+            strip = pl.ds(pl.multiple_of(part * HALF, HALF), HALF)
+            inverse = eliminate(work[strip, strip])
+            rows = full_dot(inverse, work[strip, :])
+            done[strip, :] = rows
+
+            @pl.when(part == 0)
+            def _():
+                work[HALF:, :] = work[HALF:, :] - full_dot(
+                    rows[:, HALF:B], rows, (((0,), (0,)), ((), ()))
+                )
+
+        i = lax.broadcasted_iota(jnp.int32, (B, B), 0)
+        j = lax.broadcasted_iota(jnp.int32, (B, B), 1)
+        upper = jnp.where(i <= j, done[:, :B], 0.0)
+        table[here, here] = upper.T
+        inverse_b = done[:, B:].astype(jnp.bfloat16)
+        g_rows = plain_dot(inverse_b, perm_rows).astype(jnp.bfloat16)
+        g_cols = plain_dot(inverse_b, perm_cols).astype(jnp.bfloat16)
+        g_rows_ref[step] = g_rows
+        g_cols_ref[step] = g_cols
+        pick_rows_ref[step] = plain_dot(own_rows, g_rows).astype(jnp.bfloat16)
+        pick_cols_ref[step] = plain_dot(own_cols, g_cols).astype(jnp.bfloat16)
+
+        @pl.when(step == 0)
+        def _():
+            column_b = full[B:, :B].astype(jnp.bfloat16)
+            solved = contract_last(column_b, inverse_b)
+            solved_b = solved.astype(jnp.bfloat16)
+            table[B:, :B] = solved
+            table[:B, B:] = contract_last(inverse_b, column_b)
+            full[B:, B:] = full[B:, B:] - contract_last(solved_b, solved_b)
+            transposed_in = (((0,), (0,)), ((), ()))
+            u_rows_ref[...] = lax.dot_general(
+                perm_rows, solved_b, transposed_in, preferred_element_type=jnp.float32
+            ).astype(jnp.bfloat16)
+            u_cols_ref[...] = lax.dot_general(
+                perm_cols, solved_b, transposed_in, preferred_element_type=jnp.float32
+            ).astype(jnp.bfloat16)
+
+    mine = one_hot((rows_two, wide), lambda i, j: i * row_count + row_index == j)
+    theirs = one_hot((wide, cols_two), lambda i, j: j * col_count + col_index == i)
+    corner_ref[...] = full_dot(full_dot(mine, table[...]), theirs)
+
+
+def factor_call(where, diag, row_count, col_count):
+    wide = STEPS * B
+    rows_each, cols_each = B // row_count, B // col_count
+    shape = jax.ShapeDtypeStruct
+    return pl.pallas_call(
+        functools.partial(factor_kernel, row_count, col_count),
+        out_shape=(
+            shape((STEPS, B, B), jnp.bfloat16),
+            shape((STEPS, B, B), jnp.bfloat16),
+            shape((B, B), jnp.bfloat16),
+            shape((B, B), jnp.bfloat16),
+            shape((STEPS, rows_each, B), jnp.bfloat16),
+            shape((STEPS, cols_each, B), jnp.bfloat16),
+            shape((wide // row_count, wide // col_count), jnp.float32),
+        ),
+        in_specs=[pl.BlockSpec(memory_space=pltpu.SMEM), pl.BlockSpec(memory_space=pltpu.VMEM)],
+        out_specs=tuple(pl.BlockSpec(memory_space=pltpu.VMEM) for _ in range(7)),
+        scratch_shapes=[
+            pltpu.VMEM((wide, wide), jnp.float32),
+            pltpu.VMEM((B, 2 * B), jnp.float32),
+            pltpu.VMEM((B, 2 * B), jnp.float32),
+            pltpu.VMEM((wide, wide), jnp.float32),
+        ],
+        compiler_params=pltpu.CompilerParams(vmem_limit_bytes=24 * MIB),
+        cost_estimate=pl.CostEstimate(flops=60_000_000_000, bytes_accessed=4_000_000, transcendentals=0),
+    )(where, diag)
+
+
+def update_kernel(row_tile, chunk, block_ref, rows_any, column_ref, g_rows_ref, g_cols_ref, u_rows_ref, u_cols_ref,
+                  pick_rows_ref, pick_cols_ref, corner_ref, out_ref, panel, top, side, side_b, sem):
+    index = pl.program_id(0)
+    row_count, rows_two, columns = panel.shape
+    col_count = column_ref.shape[0]
+    rows_each = rows_two // STEPS
+    cols_two = column_ref.shape[2]
+    cols_each = cols_two // STEPS
+    stride = columns // LANES
+    chunks = columns // chunk
+
+    @pl.when(index == 0)
+    def _():
+        load = pltpu.make_async_copy(rows_any, panel, sem)
+        load.start()
+        side[...] = jnp.zeros_like(side)
+        side_b[...] = jnp.zeros_like(side_b)
+
+        def piece(step):
+            return jnp.concatenate(
+                [column_ref[c, :, step * cols_each:(step + 1) * cols_each] for c in range(col_count)], axis=1
+            )
+
+        first = piece(0)
+        solved_b = contract_last(first, g_cols_ref[0]).astype(jnp.bfloat16)
+        height = column_ref.shape[1]
+        side[:height, :cols_each] = contract_last(first, pick_cols_ref[0])
+        side_b[:height, :B] = solved_b
+        second = piece(1).astype(jnp.float32) - contract_last(solved_b, u_cols_ref[...])
+        second = second.astype(jnp.bfloat16)
+        side_b[:height, B:] = contract_last(second, g_cols_ref[1]).astype(jnp.bfloat16)
+        side[:height, cols_each:] = contract_last(second, pick_cols_ref[1])
+        load.wait()
+
+        @pl.loop(0, chunks)
+        def _(at):
+            span = pl.ds(pl.multiple_of(at * chunk, chunk), chunk)
+            both = panel[:, :, span]
+            one = both[:, :rows_each, :].reshape(B, chunk)
+            two = both[:, rows_each:, :].reshape(B, chunk)
+            solved = plain_dot(g_rows_ref[0], one).astype(jnp.bfloat16)
+            top[:rows_each, span] = plain_dot(pick_rows_ref[0], one)
+            two = (two.astype(jnp.float32) - plain_dot(u_rows_ref[...], solved)).astype(jnp.bfloat16)
+            top[rows_each:, span] = plain_dot(pick_rows_ref[1], two)
+            last = plain_dot(g_rows_ref[1], two).astype(jnp.bfloat16)
+            panel[:row_count // 2, :, span] = solved.reshape(row_count // 2, rows_two, chunk)
+            panel[row_count // 2:, :, span] = last.reshape(row_count // 2, rows_two, chunk)
+
+        top[:, :cols_two] = corner_ref[...]
+
+    rows = pl.ds(pl.multiple_of(index * row_tile, row_tile), row_tile)
+    mine = side_b[rows, :]
+    first_chunks = cols_two // chunk
+
+    @pl.loop(first_chunks, chunks)
+    def _(at):
+        span = pl.ds(pl.multiple_of(at * chunk, chunk), chunk)
+        other = panel[:, :, span].reshape(STEPS * B, chunk)
+        value = block_ref[:, span].astype(jnp.float32) - plain_dot(mine, other)
+        for t in range(chunk // LANES):
+            out_ref[pl.ds(at * (chunk // LANES) + t, row_tile, stride=stride), :] = value[
+                :, t * LANES:(t + 1) * LANES
+            ]
+
+    for t in range(cols_two // LANES):
+        out_ref[pl.ds(t, row_tile, stride=stride), :] = side[rows, t * LANES:(t + 1) * LANES]
+
+    @pl.when(index == 0)
+    def _():
+        for t in range(stride):
+            out_ref[pl.ds(t, rows_two, stride=stride), :] = top[:, t * LANES:(t + 1) * LANES]
+
+
+def update_call(block, rows, column, parts, row_tile, chunk):
+    height, columns = block.shape
+    stride = columns // LANES
+    steps = pl.cdiv(height, row_tile)
+    whole = pl.BlockSpec(memory_space=pltpu.VMEM)
+    return pl.pallas_call(
+        functools.partial(update_kernel, row_tile, chunk),
+        grid=(steps,),
+        out_shape=jax.ShapeDtypeStruct((height * stride, LANES), jnp.float32),
+        in_specs=[
+            pl.BlockSpec((row_tile, columns), lambda m: (m, 0)),
+            pl.BlockSpec(memory_space=pl.ANY),
+        ] + [whole] * 8,
+        out_specs=pl.BlockSpec((row_tile * stride, LANES), lambda m: (m, 0)),
+        scratch_shapes=[
+            pltpu.VMEM(rows.shape, jnp.bfloat16),
+            pltpu.VMEM((rows.shape[1], columns), jnp.float32),
+            pltpu.VMEM((steps * row_tile, column.shape[2]), jnp.float32),
+            pltpu.VMEM((steps * row_tile, STEPS * B), jnp.bfloat16),
+            pltpu.SemaphoreType.DMA,
+        ],
+        compiler_params=pltpu.CompilerParams(vmem_limit_bytes=62 * MIB),
+        cost_estimate=pl.CostEstimate(
+            flops=2 * height * columns * STEPS * B, bytes_accessed=6 * height * columns, transcendentals=0
+        ),
+    )(block, rows, column, *parts)
+
+
+def gathered_on_device(kernel):
+    row_count = lax.axis_size("row")
+    col_count = lax.axis_size("col")
+    where = jnp.stack([lax.axis_index("row"), lax.axis_index("col")]).astype(jnp.int32)
+    work = kernel[:, 0, 0, :]
+    rows_two, cols_two = STEPS * B // row_count, STEPS * B // col_count
+    diag = lax.all_gather(work[:rows_two, :cols_two], ("row", "col"), axis=0, tiled=False)
+    diag, work = lax.optimization_barrier((diag, work))
+    rows = lax.all_gather(work[:rows_two], "row", axis=0, tiled=False)
+    column = lax.all_gather(work[:, :cols_two], "col", axis=0, tiled=False)
+    parts = factor_call(where, diag, row_count, col_count)
+    out = update_call(work, rows, column, parts, ROW_TILE, B)
+    return out.reshape(kernel.shape)
 
 
 def on_device(kernel):
@@ -70,6 +350,20 @@
 def solution(mesh):
     in_specs = (P(None, "row", "col", None),)
     out_specs = P(None, "row", "col", None)
-    return jax.shard_map(
-        on_device, mesh=mesh, in_specs=in_specs, out_specs=out_specs, check_vma=False
-    )
+    by_row, by_col = mesh.shape["row"], mesh.shape["col"]
+
+    def run(kernel):
+        height, columns = kernel.shape[0], kernel.shape[3]
+        fits = (
+            (B // by_row) % 16 == 0
+            and (B // by_col) % LANES == 0
+            and columns % B == 0
+            and height % 16 == 0
+            and height >= ROW_TILE
+        )
+        body = gathered_on_device if fits else on_device
+        return jax.shard_map(
+            body, mesh=mesh, in_specs=in_specs, out_specs=out_specs, check_vma=False
+        )(kernel)
+
+    return run

time: 614 us -> 287 us (0.47); the launches traced: 604 us -> 286 us
  other arithmetic: 167 us -> 0.08 us
  Pallas kernels: 0 us -> 160 us
  local copies, waits for them, and re-layouts: 165 us -> 9.3 us
  matrix products: 102 us -> 0 us
  blocking collectives: 154 us -> 72.7 us
  waiting for transfers between devices: 0.06 us -> 31.4 us
    pallas_call x0 -> x2, Pallas kernels: none -> 160 us  [the longest x1 85.1 us: update_call(): pl.pallas_call(functools.partial(update_kernel, row_tile, chunk), grid=(s...]
    another operation x21 -> x1, other arithmetic: 141 us -> 0.08 us  [gathered_on_device(): jnp.stack([lax.axis_index('row'), lax.axis_index('col')]).astype(jnp.int32)]
    dot_general x6 -> x0, matrix products: 95.7 us -> none  [the longest x2 76.8 us: on_device(): jnp.dot(solved_b, transposed_b, preferred_element_type=jnp.float32)]
    all_gather x4 -> x1, blocking collectives: 154 us -> 72.7 us  [gathered_on_device(): lax.all_gather(work[:rows_two, :cols_two], ('row', 'col'), axis=0, tiled=...]
    scatter x7 -> x0, local copies, waits for them, and re-layouts: 75.3 us -> none  [the longest x3 72.2 us: on_device(): work = work.at[row_start:row_end, col_end:].set(own_transposed)]
    unnamed x6 -> x14, local copies, waits for them, and re-layouts: 36.6 us -> 4.61 us
    all_gather x2, waiting for transfers between devices: 0.02 us -> 31.3 us  [the longest x1 31.3 us: gathered_on_device(): rows = lax.all_gather(work[:rows_two], 'row', axis=0, tiled=False)]
    convert_element_type x2 -> x0, other arithmetic: 26.2 us -> none  [the longest x1 26.2 us: on_device(): work = kernel[:, 0, 0, :].astype(jnp.float32)]
  transfers between devices with their start and end apart: 2 -> 2, of which waited for: 0 -> 1; matrix products, arithmetic and copies ran while one was open for 36% -> 1% of each run, Pallas kernels for 0% -> 26%
where the time goes in v1:
time: 287 us; the launch traced here: 286 us
  Pallas kernels  160 us (56%)
  blocking collectives  72.7 us (25%)
  waiting for transfers between devices  31.4 us (11%)
  between operations  13.4 us (5%)
  local copies, waits for them, and re-layouts  9.3 us (3%)
    pallas_call x1, Pallas kernels, update_call(): pl.pallas_call(functools.partial(update_kernel, row_tile, chunk), grid=(s...  85.1 us
    pallas_call x1, Pallas kernels, factor_call(): pl.pallas_call(functools.partial(factor_kernel, row_count, col_count), ou...  74.4 us
    all_gather x1, blocking collectives, gathered_on_device(): lax.all_gather(work[:rows_two, :cols_two], ('row', 'col'), axis=0, tiled=...  72.7 us
    all_gather x1, waiting for transfers between devices, gathered_on_device(): rows = lax.all_gather(work[:rows_two], 'row', axis=0, tiled=False)  31.3 us
  transfers between devices with their start and end apart: 2, of which 1 were waited for; matrix products, arithmetic and copies ran while one was open for 1% of the time, Pallas kernels for 26%

profile of v1, /device:TPU:0, one launch (start us, length us, event | category | flops | bytes accessed | tf_op | source)
XLA Modules:
  0.0 286.5 jit_solution(18300857897696876622)
XLA Ops:
  6.5 0.0 all-gather.8.cloned.1.call-start
  6.5 0.7 slice.12
  7.3 72.7 %all-gather = bf16[1024,256]{1,0:T(8,128)(2,1)S(1)} all-gather(bf16[32,256]{1,0:T(8,128)(2,1)S(1)} %slice.12), channel_id=2, replica_groups=mesh['row'=16,'col'=2] {'row','col'}, dimensions={0}, use_global_device_ids=true | all-gather | bytes 540672 | tf_op jit(solution)/shard_map/all_gather | solution.py:287
  79.9 2.0 slice.11
  81.9 0.0 all-gather.8.cloned.1.call-update
  82.0 0.0 all-gather.6.cloned.1.call-start
  82.0 2.0 slice.10
  84.0 0.0 all-gather.6.cloned.1.call-update
  84.0 0.1 pad_add_fusion.where_ref
  84.1 74.4 %shard_map.17 = (bf16[2,256,256]{2,1,0:T(8,128)(2,1)S(1)}, bf16[2,256,256]{2,1,0:T(8,128)(2,1)S(1)}, bf16[256,256]{1,0:T(8,128)(2,1)S(1)}, bf16[256,256]{1,0:T(8...) custom-call(s32[2]{0:T(128)S(1)} %pad_add_fusion.where_ref, ...), custom_call_target="tpu_custom_call" | custom-call | flops 60000002048 | bytes 4000000 | tf_op jit(solution)/shard_map/pallas_call | solution.py:156
  158.5 0.0 copy-start
  158.5 0.7 copy-done
  159.3 0.0 copy-start.1
  159.3 0.7 copy-done.1
  160.0 0.0 copy-start.2
  160.0 0.7 copy-done.2
  160.6 0.0 copy-start.3
  160.6 0.7 copy-done.3
  161.3 0.0 copy-start.4
  161.3 0.7 copy-done.4
  161.9 0.0 copy-start.5
  161.9 0.6 copy-done.5
  162.5 0.0 copy-start.6
  162.6 0.6 copy-done.6
  163.1 0.0 all-gather.8.cloned.1.call-done
  163.2 31.3 %all-gather.6.cloned.1.call-done = bf16[512,10496]{1,0:T(8,128)(2,1)} async-done(((bf16[32,10496]{1,0:T(8,128)(2,1)}), bf16[512,10496]{1,0:T(8,128)(2,1)}) %all-gather.6.cloned.1.call-update) | async-done | bytes 10747920 | tf_op jit(solution)/shard_map/all_gather | solution.py:289
  194.5 85.1 %shard_map.18 = f32[107584,128]{1,0:T(8,128)} custom-call(bf16[1312,10496]{1,0:T(8,128)(2,1)} %bitcast.11, bf16[16,32,10496]{2,1,0:T(8,128)(2,1)} %bitcast.12, bf16[2,1312,256]{2,1,0:T(8,128)(2,1)} %bitcast.13, bf16[2,256,256]{2,1,0:T(8,128)(2,1)} %copy-done, bf16[2,256,256]{2,1,0:T(8,128)(2,1)} %copy-done.1, bf16[256,256]{1,0:T(8,128)(2,1)} %copy-done.2, ...), custom_call_target="tpu_custom_call" | custom-call | flops 14101250048 | bytes 82624512 | tf_op jit(solution)/shard_map/pallas_call | solution.py:258
Async XLA Ops:
  6.5 156.6 %all-gather.8.cloned.1.call-start = ((), (), s32[]{:S(2)}) async-start(), calls=%async_computation.1 | async-start | bytes 2015232 | tf_op jit(solution)/shard_map/all_gather | solution.py:290
  82.0 112.5 %all-gather.6.cloned.1.call-start = ((), (), s32[]{:S(2)}) async-start(), calls=%async_computation | async-start | bytes 11419648 | tf_op jit(solution)/shard_map/all_gather | solution.py:289
  158.5 0.7 copy-start
  159.3 0.7 copy-start.1
  160.0 0.7 copy-start.2
  160.6 0.7 copy-start.3
  161.3 0.7 copy-start.4
  161.9 0.6 copy-start.5
  162.5 0.6 copy-start.6
Sparse Core Ops, SparseCore 0:
  82.1 20.4 all-gather.7
  104.9 89.5 all-gather.5

commit v2 on v1

--- a/solution.py
+++ b/solution.py
@@ -12,6 +12,8 @@
 HALF = 128
 LANES = 128
 ROW_TILE = 272
+CHUNK = 1024
+MESH = pl.DeviceIdType.MESH
 MIB = 1024 * 1024
 
 
@@ -64,15 +66,112 @@
     return jnp.concatenate([right[g] * lax.rsqrt(scale[g]) for g in range(groups)], axis=0)
 
 
-def factor_kernel(row_count, col_count, where_ref, diag_ref, g_rows_ref, g_cols_ref, u_rows_ref, u_cols_ref,
-                  pick_rows_ref, pick_cols_ref, corner_ref, full, work, done, table):
+def part_places(row_count, col_count):
+    sizes = (
+        ("g_rows", STEPS * B),
+        ("g_cols", STEPS * B),
+        ("u_rows", B),
+        ("u_cols", B),
+        ("pick_cols", STEPS * B // col_count),
+        ("pick_rows", STEPS * B // row_count),
+    )
+    places, at = {}, 0
+    for name, size in sizes:
+        places[name] = at
+        at += size
+    places["end"] = at
+    return places
+
+
+def exchange_kernel(row_count, block_ref, diag_ref, column_ref, local_sem, pair_send, pair_recv, send_sem, recv_sem):
+    row, col = lax.axis_index("row"), lax.axis_index("col")
+    other = 1 - col
+    rows_two, cols_two = diag_ref.shape[2], diag_ref.shape[3]
+    barrier = pltpu.get_barrier_semaphore()
+    pl.semaphore_signal(barrier, inc=1, device_id=(row, other), device_id_type=MESH)
+    for k in range(1, row_count):
+        pl.semaphore_signal(
+            barrier, inc=1, device_id=(lax.rem(row + k, row_count), col), device_id_type=MESH
+        )
+    pl.semaphore_wait(barrier, row_count)
+
+    corner = block_ref.at[pl.ds(0, rows_two), pl.ds(0, cols_two)]
+    strip = block_ref.at[:, pl.ds(0, cols_two)]
+    own_corner = pltpu.make_async_copy(corner, diag_ref.at[row, col], local_sem.at[0])
+    own_strip = pltpu.make_async_copy(strip, column_ref.at[col], local_sem.at[1])
+
+    def to_pair(source, target, which):
+        return pltpu.make_async_remote_copy(
+            src_ref=source,
+            dst_ref=target,
+            send_sem=pair_send.at[which],
+            recv_sem=pair_recv.at[which],
+            device_id=(row, other),
+            device_id_type=MESH,
+        )
+
+    def to_row(slot, k):
+        return pltpu.make_async_remote_copy(
+            src_ref=diag_ref.at[slot],
+            dst_ref=diag_ref.at[slot],
+            send_sem=send_sem.at[k],
+            recv_sem=recv_sem.at[slot],
+            device_id=(lax.rem(row + k, row_count), col),
+            device_id_type=MESH,
+        )
+
+    small = to_pair(corner, diag_ref.at[row, col], 0)
+    large = to_pair(strip, column_ref.at[col], 1)
+    small.start()
+    own_corner.start()
+    own_corner.wait()
+    to_pair(corner, diag_ref.at[row, other], 0).wait_recv()
+    sends = [to_row(row, k) for k in range(1, row_count)]
+    for copy in sends:
+        copy.start()
+    large.start()
+    own_strip.start()
+    for k in range(1, row_count):
+        to_row(lax.rem(row - k + row_count, row_count), k).wait_recv()
+    for copy in sends:
+        copy.wait_send()
+    to_pair(strip, column_ref.at[other], 1).wait_recv()
+    small.wait_send()
+    large.wait_send()
+    own_strip.wait()
+
+
+def exchange_call(block, row_count, col_count):
+    height = block.shape[0]
+    rows_two, cols_two = STEPS * B // row_count, STEPS * B // col_count
+    return pl.pallas_call(
+        functools.partial(exchange_kernel, row_count),
+        out_shape=(
+            jax.ShapeDtypeStruct((row_count, col_count, rows_two, cols_two), block.dtype),
+            jax.ShapeDtypeStruct((col_count, height, cols_two), block.dtype),
+        ),
+        in_specs=[pl.BlockSpec(memory_space=pl.ANY)],
+        out_specs=(pl.BlockSpec(memory_space=pltpu.VMEM), pl.BlockSpec(memory_space=pl.ANY)),
+        scratch_shapes=[
+            pltpu.SemaphoreType.DMA((2,)),
+            pltpu.SemaphoreType.DMA((2,)),
+            pltpu.SemaphoreType.DMA((2,)),
+            pltpu.SemaphoreType.DMA((row_count,)),
+            pltpu.SemaphoreType.DMA((row_count,)),
+        ],
+        compiler_params=pltpu.CompilerParams(collective_id=0, has_side_effects=True),
+    )(block)
+
+
+def factor_kernel(row_count, col_count, where_ref, diag_ref, parts_ref, corner_ref, full, work, done, table):
     row_index, col_index = where_ref[0], where_ref[1]
     wide = STEPS * B
     rows_each, cols_each = B // row_count, B // col_count
     rows_two, cols_two = wide // row_count, wide // col_count
+    places = part_places(row_count, col_count)
     gathered = jnp.concatenate(
         [
-            jnp.concatenate([diag_ref[r * col_count + c] for r in range(row_count)], axis=0)
+            jnp.concatenate([diag_ref[r, c] for r in range(row_count)], axis=0)
             for c in range(col_count)
         ],
         axis=1,
@@ -123,10 +222,14 @@
         inverse_b = done[:, B:].astype(jnp.bfloat16)
         g_rows = plain_dot(inverse_b, perm_rows).astype(jnp.bfloat16)
         g_cols = plain_dot(inverse_b, perm_cols).astype(jnp.bfloat16)
-        g_rows_ref[step] = g_rows
-        g_cols_ref[step] = g_cols
-        pick_rows_ref[step] = plain_dot(own_rows, g_rows).astype(jnp.bfloat16)
-        pick_cols_ref[step] = plain_dot(own_cols, g_cols).astype(jnp.bfloat16)
+
+        def place(name, size):
+            return pl.ds(pl.multiple_of(places[name] + step * size, 16), size)
+
+        parts_ref[place("g_rows", B), :] = g_rows
+        parts_ref[place("g_cols", B), :] = g_cols
+        parts_ref[place("pick_rows", rows_each), :] = plain_dot(own_rows, g_rows).astype(jnp.bfloat16)
+        parts_ref[place("pick_cols", cols_each), :] = plain_dot(own_cols, g_cols).astype(jnp.bfloat16)
 
         @pl.when(step == 0)
         def _():
@@ -137,10 +240,10 @@
             table[:B, B:] = contract_last(inverse_b, column_b)
             full[B:, B:] = full[B:, B:] - contract_last(solved_b, solved_b)
             transposed_in = (((0,), (0,)), ((), ()))
-            u_rows_ref[...] = lax.dot_general(
+            parts_ref[places["u_rows"]:places["u_rows"] + B, :] = lax.dot_general(
                 perm_rows, solved_b, transposed_in, preferred_element_type=jnp.float32
             ).astype(jnp.bfloat16)
-            u_cols_ref[...] = lax.dot_general(
+            parts_ref[places["u_cols"]:places["u_cols"] + B, :] = lax.dot_general(
                 perm_cols, solved_b, transposed_in, preferred_element_type=jnp.float32
             ).astype(jnp.bfloat16)
 
@@ -151,21 +254,15 @@
 
 def factor_call(where, diag, row_count, col_count):
     wide = STEPS * B
-    rows_each, cols_each = B // row_count, B // col_count
     shape = jax.ShapeDtypeStruct
     return pl.pallas_call(
         functools.partial(factor_kernel, row_count, col_count),
         out_shape=(
-            shape((STEPS, B, B), jnp.bfloat16),
-            shape((STEPS, B, B), jnp.bfloat16),
-            shape((B, B), jnp.bfloat16),
-            shape((B, B), jnp.bfloat16),
-            shape((STEPS, rows_each, B), jnp.bfloat16),
-            shape((STEPS, cols_each, B), jnp.bfloat16),
+            shape((part_places(row_count, col_count)["end"], B), jnp.bfloat16),
             shape((wide // row_count, wide // col_count), jnp.float32),
         ),
         in_specs=[pl.BlockSpec(memory_space=pltpu.SMEM), pl.BlockSpec(memory_space=pltpu.VMEM)],
-        out_specs=tuple(pl.BlockSpec(memory_space=pltpu.VMEM) for _ in range(7)),
+        out_specs=tuple(pl.BlockSpec(memory_space=pltpu.VMEM) for _ in range(2)),
         scratch_shapes=[
             pltpu.VMEM((wide, wide), jnp.float32),
             pltpu.VMEM((B, 2 * B), jnp.float32),
@@ -177,16 +274,27 @@
     )(where, diag)
 
 
-def update_kernel(row_tile, chunk, block_ref, rows_any, column_ref, g_rows_ref, g_cols_ref, u_rows_ref, u_cols_ref,
-                  pick_rows_ref, pick_cols_ref, corner_ref, out_ref, panel, top, side, side_b, sem):
+def update_kernel(row_tile, places, block_ref, rows_any, column_ref, parts_ref, corner_ref, out_ref, panel, top,
+                  side, side_b, sem):
     index = pl.program_id(0)
     row_count, rows_two, columns = panel.shape
-    col_count = column_ref.shape[0]
+    col_count, height, cols_two = column_ref.shape
     rows_each = rows_two // STEPS
-    cols_two = column_ref.shape[2]
     cols_each = cols_two // STEPS
     stride = columns // LANES
-    chunks = columns // chunk
+    chunks = columns // CHUNK
+
+    def part(name, size, step=0):
+        begin = places[name] + step * size
+        return parts_ref[begin:begin + size, :]
+
+    def over_columns(body):
+        @pl.loop(0, chunks)
+        def _(at):
+            body(pl.multiple_of(at * CHUNK, CHUNK), CHUNK)
+
+        if columns % CHUNK:
+            body(chunks * CHUNK, columns % CHUNK)
 
     @pl.when(index == 0)
     def _():
@@ -201,46 +309,43 @@
             )
 
         first = piece(0)
-        solved_b = contract_last(first, g_cols_ref[0]).astype(jnp.bfloat16)
-        height = column_ref.shape[1]
-        side[:height, :cols_each] = contract_last(first, pick_cols_ref[0])
+        solved_b = contract_last(first, part("g_cols", B)).astype(jnp.bfloat16)
+        side[:height, :cols_each] = contract_last(first, part("pick_cols", cols_each))
         side_b[:height, :B] = solved_b
-        second = piece(1).astype(jnp.float32) - contract_last(solved_b, u_cols_ref[...])
+        second = piece(1).astype(jnp.float32) - contract_last(solved_b, part("u_cols", B))
         second = second.astype(jnp.bfloat16)
-        side_b[:height, B:] = contract_last(second, g_cols_ref[1]).astype(jnp.bfloat16)
-        side[:height, cols_each:] = contract_last(second, pick_cols_ref[1])
+        side_b[:height, B:] = contract_last(second, part("g_cols", B, 1)).astype(jnp.bfloat16)
+        side[:height, cols_each:] = contract_last(second, part("pick_cols", cols_each, 1))
         load.wait()
 
-        @pl.loop(0, chunks)
-        def _(at):
-            span = pl.ds(pl.multiple_of(at * chunk, chunk), chunk)
+        def solve(start, width):
+            span = pl.ds(start, width)
             both = panel[:, :, span]
-            one = both[:, :rows_each, :].reshape(B, chunk)
-            two = both[:, rows_each:, :].reshape(B, chunk)
-            solved = plain_dot(g_rows_ref[0], one).astype(jnp.bfloat16)
-            top[:rows_each, span] = plain_dot(pick_rows_ref[0], one)
-            two = (two.astype(jnp.float32) - plain_dot(u_rows_ref[...], solved)).astype(jnp.bfloat16)
-            top[rows_each:, span] = plain_dot(pick_rows_ref[1], two)
-            last = plain_dot(g_rows_ref[1], two).astype(jnp.bfloat16)
-            panel[:row_count // 2, :, span] = solved.reshape(row_count // 2, rows_two, chunk)
-            panel[row_count // 2:, :, span] = last.reshape(row_count // 2, rows_two, chunk)
-
+            one = both[:, :rows_each, :].reshape(B, width)
+            two = both[:, rows_each:, :].reshape(B, width)
+            solved = plain_dot(part("g_rows", B), one).astype(jnp.bfloat16)
+            top[:rows_each, span] = plain_dot(part("pick_rows", rows_each), one)
+            two = (two.astype(jnp.float32) - plain_dot(part("u_rows", B), solved)).astype(jnp.bfloat16)
+            top[rows_each:, span] = plain_dot(part("pick_rows", rows_each, 1), two)
+            last = plain_dot(part("g_rows", B, 1), two).astype(jnp.bfloat16)
+            panel[:row_count // 2, :, span] = solved.reshape(row_count // 2, rows_two, width)
+            panel[row_count // 2:, :, span] = last.reshape(row_count // 2, rows_two, width)
+
+        over_columns(solve)
         top[:, :cols_two] = corner_ref[...]
 
     rows = pl.ds(pl.multiple_of(index * row_tile, row_tile), row_tile)
-    mine = side_b[rows, :]
-    first_chunks = cols_two // chunk
-
-    @pl.loop(first_chunks, chunks)
-    def _(at):
-        span = pl.ds(pl.multiple_of(at * chunk, chunk), chunk)
-        other = panel[:, :, span].reshape(STEPS * B, chunk)
-        value = block_ref[:, span].astype(jnp.float32) - plain_dot(mine, other)
-        for t in range(chunk // LANES):
-            out_ref[pl.ds(at * (chunk // LANES) + t, row_tile, stride=stride), :] = value[
+
+    def subtract(start, width):
+        span = pl.ds(start, width)
+        other = panel[:, :, span].reshape(STEPS * B, width)
+        value = block_ref[:, span].astype(jnp.float32) - plain_dot(side_b[rows, :], other)
+        for t in range(width // LANES):
+            out_ref[pl.ds(start // LANES + t, row_tile, stride=stride), :] = value[
                 :, t * LANES:(t + 1) * LANES
             ]
 
+    over_columns(subtract)
     for t in range(cols_two // LANES):
         out_ref[pl.ds(t, row_tile, stride=stride), :] = side[rows, t * LANES:(t + 1) * LANES]
 
@@ -250,19 +355,19 @@
             out_ref[pl.ds(t, rows_two, stride=stride), :] = top[:, t * LANES:(t + 1) * LANES]
 
 
-def update_call(block, rows, column, parts, row_tile, chunk):
+def update_call(block, rows, column, parts, corner, places, row_tile):
     height, columns = block.shape
     stride = columns // LANES
     steps = pl.cdiv(height, row_tile)
     whole = pl.BlockSpec(memory_space=pltpu.VMEM)
     return pl.pallas_call(
-        functools.partial(update_kernel, row_tile, chunk),
+        functools.partial(update_kernel, row_tile, places),
         grid=(steps,),
         out_shape=jax.ShapeDtypeStruct((height * stride, LANES), jnp.float32),
         in_specs=[
             pl.BlockSpec((row_tile, columns), lambda m: (m, 0)),
             pl.BlockSpec(memory_space=pl.ANY),
-        ] + [whole] * 8,
+        ] + [whole] * 3,
         out_specs=pl.BlockSpec((row_tile * stride, LANES), lambda m: (m, 0)),
         scratch_shapes=[
             pltpu.VMEM(rows.shape, jnp.bfloat16),
@@ -275,7 +380,7 @@
         cost_estimate=pl.CostEstimate(
             flops=2 * height * columns * STEPS * B, bytes_accessed=6 * height * columns, transcendentals=0
         ),
-    )(block, rows, column, *parts)
+    )(block, rows, column, parts, corner)
 
 
 def gathered_on_device(kernel):
@@ -283,13 +388,10 @@
     col_count = lax.axis_size("col")
     where = jnp.stack([lax.axis_index("row"), lax.axis_index("col")]).astype(jnp.int32)
     work = kernel[:, 0, 0, :]
-    rows_two, cols_two = STEPS * B // row_count, STEPS * B // col_count
-    diag = lax.all_gather(work[:rows_two, :cols_two], ("row", "col"), axis=0, tiled=False)
-    diag, work = lax.optimization_barrier((diag, work))
-    rows = lax.all_gather(work[:rows_two], "row", axis=0, tiled=False)
-    column = lax.all_gather(work[:, :cols_two], "col", axis=0, tiled=False)
-    parts = factor_call(where, diag, row_count, col_count)
-    out = update_call(work, rows, column, parts, ROW_TILE, B)
+    rows = lax.all_gather(work[:STEPS * B // row_count], "row", axis=0, tiled=False)
+    diag, column = exchange_call(work, row_count, col_count)
+    parts, corner = factor_call(where, diag, row_count, col_count)
+    out = update_call(work, rows, column, parts, corner, part_places(row_count, col_count), ROW_TILE)
     return out.reshape(kernel.shape)
 
 
@@ -357,6 +459,7 @@
         fits = (
             (B // by_row) % 16 == 0
             and (B // by_col) % LANES == 0
+            and by_col == 2
             and columns % B == 0
             and height % 16 == 0
             and height >= ROW_TILE

time: 287 us -> 173 us (0.60)
  blocking collectives: 72.7 us -> 0 us
  waiting for transfers between devices: 31.4 us -> 0.02 us
  Pallas kernels: 160 us -> 155 us
  local copies, waits for them, and re-layouts: 9.3 us -> 4.61 us
    all_gather x1 -> x0, blocking collectives: 72.7 us -> none  [gathered_on_device(): lax.all_gather(work[:rows_two, :cols_two], ('row', 'col'), axis=0, tiled=...]
    all_gather x2 -> x1, waiting for transfers between devices: 31.3 us -> 0.01 us  [gathered_on_device(): lax.all_gather(work[:STEPS * B // row_count], 'row', axis=0, tiled=False)]
    pallas_call x1 -> x2, Pallas kernels: 85.1 us -> 80.4 us  [the longest x1 48.3 us: update_call(): pl.pallas_call(functools.partial(update_kernel, row_tile, places), grid=(...]
  transfers between devices with their start and end apart: 2 -> 1, of which waited for: 1 -> 0; matrix products, arithmetic and copies ran while one was open for 1% -> 0% of each run, Pallas kernels for 26% -> 62%
where the time goes in v2:
time: 173 us
  Pallas kernels  155 us (90%)
  between operations  13.4 us (8%)
  local copies, waits for them, and re-layouts  4.61 us (3%)
    pallas_call x1, Pallas kernels, factor_call(): pl.pallas_call(functools.partial(factor_kernel, row_count, col_count), ou...  74.5 us
    pallas_call x1, Pallas kernels, update_call(): pl.pallas_call(functools.partial(update_kernel, row_tile, places), grid=(...  48.3 us
    pallas_call x1, Pallas kernels, exchange_call(): pl.pallas_call(functools.partial(exchange_kernel, row_count), out_shape=(...  32.1 us
  transfers between devices with their start and end apart: 1, of which 0 were waited for; matrix products, arithmetic and copies ran while one was open for 0% of the time, Pallas kernels for 62%

profile of v2, /device:TPU:0, one launch (start us, length us, event | category | flops | bytes accessed | tf_op | source)
XLA Modules:
  0.0 173.1 jit_solution(8629164500321361826)
XLA Ops:
  6.5 0.0 all-gather.3.cloned.1.call-start
  6.5 2.0 %slice.4 = bf16[32,1,1,10496]{3,0,2,1:T(8,128)(2,1)} slice(bf16[1312,1,1,10496]{3,0,2,1:T(8,128)(2,1)} %param.1), slice={[0:32], [0:1], [0:1], [0:10496]} | slice | bytes 1343488 | tf_op jit(solution)/shard_map/slice | solution.py:391
  8.5 0.0 all-gather.3.cloned.1.call-update
  8.5 32.1 %shard_map.17 = (bf16[16,2,32,256]{3,2,1,0:T(8,128)(2,1)}, bf16[2,1312,256]{2,1,0:T(8,128)(2,1)}) custom-call(bf16[1312,10496]{1,0:T(8,128)(2,1)} %bitcast.5), custom_call_target="tpu_custom_call" | custom-call | tf_op jit(solution)/shard_map/pallas_call | solution.py:147
  40.6 0.1 pad_add_fusion.where_ref
  40.7 0.0 copy-start.2
  40.7 1.0 copy-done.2
  41.7 74.5 %shard_map.18 = (bf16[1824,256]{1,0:T(8,128)(2,1)S(1)}, f32[32,256]{1,0:T(8,128)S(1)}) custom-call(s32[2]{0:T(128)S(1)} %pad_add_fusion.where_ref, bf16[16,2,32,256]{3,2,1,0:T(8,128)(2,1)S(1)} %copy-done.2), custom_call_target="tpu_custom_call" | custom-call | flops 60000002048 | bytes 4000000 | tf_op jit(solution)/shard_map/pallas_call | solution.py:258
  116.3 0.0 copy-start
  116.3 1.0 copy-done
  117.3 0.0 copy-start.1
  117.3 0.6 copy-done.1
  117.9 0.0 all-gather.3.cloned.1.call-done
  117.9 48.3 %shard_map.19 = f32[107584,128]{1,0:T(8,128)} custom-call(bf16[1312,10496]{1,0:T(8,128)(2,1)} %bitcast.6, bf16[16,32,10496]{2,1,0:T(8,128)(2,1)} %bitcast.7, bf16[2,1312,256]{2,1,0:T(8,128)(2,1)} %get-tuple-element.9.column_ref, bf16[1824,256]{1,0:T(8,128)(2,1)} %copy-done, f32[32,256]{1,0:T(8,128)} %copy-done.1), custom_call_target="tpu_custom_call" | custom-call | flops 14101250048 | bytes 82624512 | tf_op jit(solution)/shard_map/pallas_call | solution.py:363
Async XLA Ops:
  6.5 111.3 %all-gather.3.cloned.1.call-start = ((), (), s32[]{:S(2)}) async-start(), calls=%async_computation | async-start | bytes 11419648 | tf_op jit(solution)/shard_map/all_gather | solution.py:391
  40.7 1.0 copy-start.2
  116.3 1.0 copy-start
  117.3 0.6 copy-start.1
Sparse Core Ops, SparseCore 0:
  9.6 96.7 all-gather.2

commit v3 on v2

--- a/solution.py
+++ b/solution.py
@@ -46,23 +46,32 @@
     left = [block[8 * g:8 * g + 8, :] for g in range(groups)]
     right = [jnp.where(lane == sub + 8 * g, 1.0, 0.0) for g in range(groups)]
     scale = [jnp.zeros((8, LANES), jnp.float32) for _ in range(groups)]
-    for k in range(HALF):
+    for k in range(0, HALF, 2):
         g, s = divmod(k, 8)
         row_left = jnp.broadcast_to(left[g][s:s + 1, :], (8, LANES))
         row_right = jnp.broadcast_to(right[g][s:s + 1, :], (8, LANES))
+        next_left = jnp.broadcast_to(left[g][s + 1:s + 2, :], (8, LANES))
+        next_right = jnp.broadcast_to(right[g][s + 1:s + 2, :], (8, LANES))
         pivot = jnp.broadcast_to(row_left[:, k:k + 1], (8, LANES))
-        scale[g] = jnp.where(sub == s, pivot, scale[g])
+        cross = jnp.broadcast_to(next_left[:, k:k + 1], (8, LANES))
+        corner = jnp.broadcast_to(next_left[:, k + 1:k + 2], (8, LANES))
         inverse = 1.0 / pivot
+        ratio = cross * inverse
+        second = corner - cross * ratio
+        inverse_second = 1.0 / second
+        scale[g] = jnp.where(sub == s, pivot, jnp.where(sub == s + 1, second, scale[g]))
+        next_left = (next_left - ratio * row_left) * inverse_second
+        next_right = (next_right - ratio * row_right) * inverse_second
         row_left = row_left * inverse
         row_right = row_right * inverse
         for u in range(g, groups):
-            if u == g and s == 7:
-                continue
             column = jnp.broadcast_to(left[u][:, k:k + 1], (8, LANES))
+            following = jnp.broadcast_to(left[u][:, k + 1:k + 2], (8, LANES)) - column * ratio
             if u == g:
                 column = jnp.where(sub > s, column, 0.0)
-            left[u] = left[u] - column * row_left
-            right[u] = right[u] - column * row_right
+                following = jnp.where(sub > s + 1, following, 0.0)
+            left[u] = left[u] - column * row_left - following * next_left
+            right[u] = right[u] - column * row_right - following * next_right
     return jnp.concatenate([right[g] * lax.rsqrt(scale[g]) for g in range(groups)], axis=0)
 
 
@@ -274,51 +283,80 @@
     )(where, diag)
 
 
-def update_kernel(row_tile, places, block_ref, rows_any, column_ref, parts_ref, corner_ref, out_ref, panel, top,
-                  side, side_b, sem):
-    index = pl.program_id(0)
-    row_count, rows_two, columns = panel.shape
+def side_kernel(places, column_ref, parts_ref, side_ref, side_b_ref):
     col_count, height, cols_two = column_ref.shape
-    rows_each = rows_two // STEPS
     cols_each = cols_two // STEPS
-    stride = columns // LANES
-    chunks = columns // CHUNK
 
     def part(name, size, step=0):
         begin = places[name] + step * size
         return parts_ref[begin:begin + size, :]
 
+    def piece(step):
+        return jnp.concatenate(
+            [column_ref[c, :, step * cols_each:(step + 1) * cols_each] for c in range(col_count)], axis=1
+        )
+
+    side_ref[...] = jnp.zeros_like(side_ref)
+    side_b_ref[...] = jnp.zeros_like(side_b_ref)
+    first = piece(0)
+    solved_b = contract_last(first, part("g_cols", B)).astype(jnp.bfloat16)
+    side_ref[:height, :cols_each] = contract_last(first, part("pick_cols", cols_each))
+    side_b_ref[:height, :B] = solved_b
+    second = piece(1).astype(jnp.float32) - contract_last(solved_b, part("u_cols", B))
+    second = second.astype(jnp.bfloat16)
+    side_b_ref[:height, B:] = contract_last(second, part("g_cols", B, 1)).astype(jnp.bfloat16)
+    side_ref[:height, cols_each:] = contract_last(second, part("pick_cols", cols_each, 1))
+
+
+def side_call(column, parts, places, row_tile):
+    height = pl.cdiv(column.shape[1], row_tile) * row_tile
+    return pl.pallas_call(
+        functools.partial(side_kernel, places),
+        out_shape=(
+            jax.ShapeDtypeStruct((height, column.shape[2]), jnp.float32),
+            jax.ShapeDtypeStruct((height, STEPS * B), jnp.bfloat16),
+        ),
+        in_specs=[pl.BlockSpec(memory_space=pltpu.VMEM)] * 2,
+        out_specs=(pl.BlockSpec(memory_space=pltpu.VMEM),) * 2,
+        compiler_params=pltpu.CompilerParams(vmem_limit_bytes=32 * MIB),
+        cost_estimate=pl.CostEstimate(flops=6_000_000_000, bytes_accessed=8_000_000, transcendentals=0),
+    )(column, parts)
+
+
+def update_kernel(row_tile, places, block_ref, rows_any, side_ref, side_b_ref, parts_ref, corner_ref, out_ref, panel,
+                  top, sem):
+    index = pl.program_id(0)
+    row_count, rows_two, columns = panel.shape
+    cols_two = side_ref.shape[1]
+    rows_each = rows_two // STEPS
+    stride = columns // LANES
+    chunks = columns // CHUNK
+
+    def part(name, size, step=0):
+        begin = places[name] + step * size
+        return parts_ref[begin:begin + size, :]
+
     def over_columns(body):
         @pl.loop(0, chunks)
         def _(at):
-            body(pl.multiple_of(at * CHUNK, CHUNK), CHUNK)
+            body(at, pl.multiple_of(at * CHUNK, CHUNK), CHUNK)
 
         if columns % CHUNK:
-            body(chunks * CHUNK, columns % CHUNK)
+            body(chunks, chunks * CHUNK, columns % CHUNK)
 
     @pl.when(index == 0)
     def _():
-        load = pltpu.make_async_copy(rows_any, panel, sem)
-        load.start()
-        side[...] = jnp.zeros_like(side)
-        side_b[...] = jnp.zeros_like(side_b)
-
-        def piece(step):
-            return jnp.concatenate(
-                [column_ref[c, :, step * cols_each:(step + 1) * cols_each] for c in range(col_count)], axis=1
-            )
-
-        first = piece(0)
-        solved_b = contract_last(first, part("g_cols", B)).astype(jnp.bfloat16)
-        side[:height, :cols_each] = contract_last(first, part("pick_cols", cols_each))
-        side_b[:height, :B] = solved_b
-        second = piece(1).astype(jnp.float32) - contract_last(solved_b, part("u_cols", B))
-        second = second.astype(jnp.bfloat16)
-        side_b[:height, B:] = contract_last(second, part("g_cols", B, 1)).astype(jnp.bfloat16)
-        side[:height, cols_each:] = contract_last(second, part("pick_cols", cols_each, 1))
-        load.wait()
-
-        def solve(start, width):
+        def load(at, start, width):
+            span = pl.ds(start, width)
+            return pltpu.make_async_copy(rows_any.at[:, :, span], panel.at[:, :, span], sem.at[at])
+
+        def begin(at, start, width):
+            load(at, start, width).start()
+
+        over_columns(begin)
+
+        def solve(at, start, width):
+            load(at, start, width).wait()
             span = pl.ds(start, width)
             both = panel[:, :, span]
             one = both[:, :rows_each, :].reshape(B, width)
@@ -334,12 +372,10 @@
         over_columns(solve)
         top[:, :cols_two] = corner_ref[...]
 
-    rows = pl.ds(pl.multiple_of(index * row_tile, row_tile), row_tile)
-
-    def subtract(start, width):
+    def subtract(at, start, width):
         span = pl.ds(start, width)
         other = panel[:, :, span].reshape(STEPS * B, width)
-        value = block_ref[:, span].astype(jnp.float32) - plain_dot(side_b[rows, :], other)
+        value = block_ref[:, span].astype(jnp.float32) - plain_dot(side_b_ref[...], other)
         for t in range(width // LANES):
             out_ref[pl.ds(start // LANES + t, row_tile, stride=stride), :] = value[
                 :, t * LANES:(t + 1) * LANES
@@ -347,7 +383,7 @@
 
     over_columns(subtract)
     for t in range(cols_two // LANES):
-        out_ref[pl.ds(t, row_tile, stride=stride), :] = side[rows, t * LANES:(t + 1) * LANES]
+        out_ref[pl.ds(t, row_tile, stride=stride), :] = side_ref[:, t * LANES:(t + 1) * LANES]
 
     @pl.when(index == 0)
     def _():
@@ -355,7 +391,7 @@
             out_ref[pl.ds(t, rows_two, stride=stride), :] = top[:, t * LANES:(t + 1) * LANES]
 
 
-def update_call(block, rows, column, parts, corner, places, row_tile):
+def update_call(block, rows, side, side_b, parts, corner, places, row_tile):
     height, columns = block.shape
     stride = columns // LANES
     steps = pl.cdiv(height, row_tile)
@@ -367,20 +403,22 @@
         in_specs=[
             pl.BlockSpec((row_tile, columns), lambda m: (m, 0)),
             pl.BlockSpec(memory_space=pl.ANY),
-        ] + [whole] * 3,
+            pl.BlockSpec((row_tile, side.shape[1]), lambda m: (m, 0)),
+            pl.BlockSpec((row_tile, side_b.shape[1]), lambda m: (m, 0)),
+            whole,
+            whole,
+        ],
         out_specs=pl.BlockSpec((row_tile * stride, LANES), lambda m: (m, 0)),
         scratch_shapes=[
             pltpu.VMEM(rows.shape, jnp.bfloat16),
             pltpu.VMEM((rows.shape[1], columns), jnp.float32),
-            pltpu.VMEM((steps * row_tile, column.shape[2]), jnp.float32),
-            pltpu.VMEM((steps * row_tile, STEPS * B), jnp.bfloat16),
-            pltpu.SemaphoreType.DMA,
+            pltpu.SemaphoreType.DMA((pl.cdiv(columns, CHUNK),)),
         ],
         compiler_params=pltpu.CompilerParams(vmem_limit_bytes=62 * MIB),
         cost_estimate=pl.CostEstimate(
             flops=2 * height * columns * STEPS * B, bytes_accessed=6 * height * columns, transcendentals=0
         ),
-    )(block, rows, column, parts, corner)
+    )(block, rows, side, side_b, parts, corner)
 
 
 def gathered_on_device(kernel):
@@ -391,7 +429,9 @@
     rows = lax.all_gather(work[:STEPS * B // row_count], "row", axis=0, tiled=False)
     diag, column = exchange_call(work, row_count, col_count)
     parts, corner = factor_call(where, diag, row_count, col_count)
-    out = update_call(work, rows, column, parts, corner, part_places(row_count, col_count), ROW_TILE)
+    places = part_places(row_count, col_count)
+    side, side_b = side_call(column, parts, places, ROW_TILE)
+    out = update_call(work, rows, side, side_b, parts, corner, places, ROW_TILE)
     return out.reshape(kernel.shape)
 
 

time: 173 us -> 160 us (0.925)
  Pallas kernels: 155 us -> 124 us
  waiting for transfers between devices: 0.02 us -> 16.7 us
    pallas_call x1, Pallas kernels: 74.5 us -> 44.1 us  [factor_call(): pl.pallas_call(functools.partial(factor_kernel, row_count, col_count), ou...]
    all_gather x1, waiting for transfers between devices: 0.01 us -> 16.7 us  [gathered_on_device(): lax.all_gather(work[:STEPS * B // row_count], 'row', axis=0, tiled=False)]
    pallas_call x1, Pallas kernels: 48.3 us -> 46.4 us  [update_call(): pl.pallas_call(functools.partial(update_kernel, row_tile, places), grid=(...]
    unnamed x6 -> x12, local copies, waits for them, and re-layouts: 2.63 us -> 3.89 us
  transfers between devices with their start and end apart: 1 -> 1, of which waited for: 0 -> 1; matrix products, arithmetic and copies ran while one was open for 0% -> 0% of each run, Pallas kernels for 62% -> 48%
where the time goes in v3:
time: 160 us
  Pallas kernels  124 us (78%)
  waiting for transfers between devices  16.7 us (10%)
  between operations  13.4 us (8%)
  local copies, waits for them, and re-layouts  5.87 us (4%)
    pallas_call x1, Pallas kernels, update_call(): pl.pallas_call(functools.partial(update_kernel, row_tile, places), grid=(...  46.4 us
    pallas_call x1, Pallas kernels, factor_call(): pl.pallas_call(functools.partial(factor_kernel, row_count, col_count), ou...  44.1 us
    pallas_call x1, Pallas kernels, exchange_call(): pl.pallas_call(functools.partial(exchange_kernel, row_count), out_shape=(...  32.1 us
    all_gather x1, waiting for transfers between devices, gathered_on_device(): lax.all_gather(work[:STEPS * B // row_count], 'row', axis=0, tiled=False)  16.7 us
    unnamed x12, local copies, waits for them, and re-layouts  3.89 us
  transfers between devices with their start and end apart: 1, of which 1 were waited for; matrix products, arithmetic and copies ran while one was open for 0% of the time, Pallas kernels for 48%

profile of v3, /device:TPU:0, one launch (start us, length us, event | category | flops | bytes accessed | tf_op | source)
XLA Modules:
  0.0 159.7 jit_solution(3826448047548029369)
XLA Ops:
  6.5 0.0 all-gather.3.cloned.1.call-start
  6.5 2.0 %slice.4 = bf16[32,1,1,10496]{3,0,2,1:T(8,128)(2,1)} slice(bf16[1312,1,1,10496]{3,0,2,1:T(8,128)(2,1)} %param.1), slice={[0:32], [0:1], [0:1], [0:10496]} | slice | bytes 1343488 | tf_op jit(solution)/shard_map/slice | solution.py:429
  8.5 0.0 all-gather.3.cloned.1.call-update
  8.5 32.1 %shard_map.17 = (bf16[16,2,32,256]{3,2,1,0:T(8,128)(2,1)}, bf16[2,1312,256]{2,1,0:T(8,128)(2,1)}) custom-call(bf16[1312,10496]{1,0:T(8,128)(2,1)} %bitcast.5), custom_call_target="tpu_custom_call" | custom-call | tf_op jit(solution)/shard_map/pallas_call | solution.py:156
  40.6 0.1 pad_add_fusion.where_ref
  40.7 0.0 copy-start.5
  40.7 1.0 copy-done.5
  41.7 0.0 copy-start.4
  41.7 44.1 %shard_map.18 = (bf16[1824,256]{1,0:T(8,128)(2,1)S(1)}, f32[32,256]{1,0:T(8,128)S(1)}) custom-call(s32[2]{0:T(128)S(1)} %pad_add_fusion.where_ref, bf16[16,2,32,256]{3,2,1,0:T(8,128)(2,1)S(1)} %copy-done.5), custom_call_target="tpu_custom_call" | custom-call | flops 60000002048 | bytes 4000000 | tf_op jit(solution)/shard_map/pallas_call | solution.py:267
  85.8 0.0 copy-start.3
  85.8 0.6 copy-done.3
  86.5 0.0 copy-start.2
  86.5 0.0 copy-done.4
  86.5 1.0 shard_map.19
  87.5 0.0 copy-done.2
  87.5 0.0 copy-start
  87.5 1.1 copy-done
  88.6 0.0 copy-start.1
  88.6 1.1 copy-done.1
  89.8 16.7 %all-gather.3.cloned.1.call-done = bf16[512,1,1,10496]{3,0,2,1:T(8,128)(2,1)} async-done(((bf16[32,1,1,10496]{3,0,2,1:T(8,128)(2,1)}), bf16[512,1,1,10496]{3,0,2,1:T(8,128)(2,1)}) %all-gather.3.cloned.1.call-update) | async-done | bytes 10747920 | tf_op jit(solution)/shard_map/all_gather | solution.py:429
  106.5 46.4 %shard_map.20 = f32[107584,128]{1,0:T(8,128)} custom-call(bf16[1312,10496]{1,0:T(8,128)(2,1)} %bitcast.6, bf16[16,32,10496]{2,1,0:T(8,128)(2,1)} %bitcast.7, f32[1360,256]{1,0:T(8,128)} %copy-done, bf16[1360,512]{1,0:T(8,128)(2,1)} %copy-done.1, bf16[1824,256]{1,0:T(8,128)(2,1)} %copy-done.2, f32[32,256]{1,0:T(8,128)} %copy-done.3), custom_call_target="tpu_custom_call" | custom-call | flops 14101250048 | bytes 82624512 | tf_op jit(solution)/shard_map/pallas_call | solution.py:399
Async XLA Ops:
  6.5 99.9 %all-gather.3.cloned.1.call-start = ((), (), s32[]{:S(2)}) async-start(), calls=%async_computation | async-start | bytes 11419648 | tf_op jit(solution)/shard_map/all_gather | solution.py:429
  40.7 1.0 copy-start.5
  41.7 44.7 %copy-start.4 = (bf16[2,1312,256]{2,1,0:T(8,128)(2,1)S(1)}, bf16[2,1312,256]{2,1,0:T(8,128)(2,1)}, u32[]{:S(2)}) copy-start(bf16[2,1312,256]{2,1,0:T(8,128)(2,1)} %get-tuple-element.11.column_ref) | copy-start | bytes 4030468
  85.8 0.6 copy-start.3
  86.5 1.1 copy-start.2
  87.5 1.1 copy-start
  88.6 1.1 copy-start.1
Sparse Core Ops, SparseCore 0:
  9.6 96.7 all-gather.2
